TPU v7x, 32 devices: a whole 2x2x4 slice. The times are simulated.
32 devices in a mesh: group: 2 (over x), dev: 16 (over z, y, core).
Axes of the slice: x: 2, y: 2, z: 4, core: 2. Of those that a mesh axis runs over, the one named last changes fastest.
Arguments:
- queries: bfloat16 [128, 4096], P(('group', 'dev')), parts along dimension 0, may hold values from -6 to 6
- cache_keys: bfloat16 [128, 512, 256], P(('group', 'dev')), parts along dimension 0, may hold values from -4 to 4
- cache_values: bfloat16 [128, 512, 256], P(('group', 'dev')), parts along dimension 0, may hold values from -6 to 6
- row_lengths: int32 [128], P(('group', 'dev')), parts along dimension 0, may hold values from 2 to 512, as said below
- residual: bfloat16 [128, 7168], P(('group', 'dev')), parts along dimension 0, may hold values from -6 to 6
- out_weight: bfloat16 [16, 1024, 1792], P('dev'), may hold values from -0.3125 to 0.3125
- norm_gain: float32 [7168], replicated, may hold values from 0.1 to 1.9
- expert_ids: int32 [128, 3], P(('group', 'dev')), parts along dimension 0, may hold values from 0 to 3, all different within a row
- gate_scores: float32 [128, 3], P(('group', 'dev')), parts along dimension 0, may hold values from -6 to 6
- gate_weight: bfloat16 [7168, 10240], P(None, 'dev'), may hold values from -0.0625 to 0.0625
- up_weight: bfloat16 [7168, 10240], P(None, 'dev'), may hold values from -0.0625 to 0.0625
- down_weight: bfloat16 [16, 2560, 1792], P('dev'), may hold values from -0.125 to 0.125
Outputs:
- layer_out: bfloat16 [128, 7168], P(('group', 'dev')), parts along dimension 0
There are 2 independent parts, one for each index of `group`. A program takes and returns all parts, laid end to end along the dimension named above; an argument that names none is the same for every part. Nothing has to cross between parts.
Inputs may be any that keep to these rules, and one draw needn't show every extreme that they name: `row_lengths`: each request's cache is live from position 0 up to its length; some request of the part has all 512 positions live.
All inputs are finite; a program needn't handle non-finite values.
Results may differ from a plain program's by a relative error of at most 0.012.
Values may be sent and summed in bfloat16 or wider, within the bound.
A program may use at most 64 MiB of HBM per device.

v0:
```python
import jax
import jax.numpy as jnp
from jax import lax
from jax.sharding import PartitionSpec as P

EXPERTS = 4
COLS = 4


def fold_blocks(received, splits, rows_here, row_scale):
    shaped = received.reshape(splits, COLS, rows_here, received.shape[2])
    if row_scale is not None:
        shaped = shaped * row_scale[:, None, :, None]
    summed = jnp.sum(shaped, axis=0)
    return jnp.transpose(summed, (1, 0, 2)).reshape(rows_here, COLS * received.shape[2])


def body(
    queries,
    cache_keys,
    cache_values,
    row_lengths,
    residual,
    out_weight,
    norm_gain,
    expert_ids,
    gate_scores,
    gate_weight,
    up_weight,
    down_weight,
):
    rows_here = queries.shape[0]
    head_dim = cache_keys.shape[2]
    head_count = queries.shape[1] // head_dim
    cache_len = cache_keys.shape[1]
    devices = lax.axis_size("dev")
    splits = devices // COLS
    blocks_each = splits // EXPERTS
    query_heads = queries.reshape(rows_here, head_count, head_dim)
    scores = jnp.einsum(
        "rhc,rlc->rhl", query_heads, cache_keys, preferred_element_type=jnp.float32
    ) * head_dim ** (-0.5)
    positions = jnp.arange(cache_len, dtype=jnp.int32)
    is_live = (positions[None, :] < row_lengths[:, None])[:, None, :]
    masked = jnp.where(is_live, scores, -1e30)
    largest = jnp.max(masked, axis=-1, keepdims=True)
    exponent = jnp.where(is_live, jnp.exp(masked - largest), 0.0)
    attn_probs = (exponent / jnp.sum(exponent, axis=-1, keepdims=True)).astype(jnp.bfloat16)
    context = jnp.einsum(
        "rhl,rlc->rhc", attn_probs, cache_values, preferred_element_type=jnp.float32
    ).astype(jnp.bfloat16)
    head_blocks = jnp.transpose(
        context.reshape(rows_here, splits, head_count // splits * head_dim), (1, 0, 2)
    )
    outgoing = jnp.repeat(head_blocks, COLS, axis=0)
    gathered = lax.all_to_all(outgoing, "dev", split_axis=0, concat_axis=0, tiled=True)
    context_rows = gathered.reshape(devices * rows_here, gathered.shape[2])
    head_part = jnp.dot(context_rows, out_weight[0], preferred_element_type=jnp.float32)
    returned_heads = lax.all_to_all(
        head_part.reshape(devices, rows_here, head_part.shape[1]).astype(jnp.bfloat16),
        "dev",
        split_axis=0,
        concat_axis=0,
        tiled=True,
    ).astype(jnp.float32)
    attended = residual.astype(jnp.float32) + fold_blocks(returned_heads, splits, rows_here, None)
    mean_square = jnp.mean(attended * attended, axis=-1, keepdims=True)
    normed = (attended * lax.rsqrt(mean_square + 1e-05) * norm_gain[None, :]).astype(jnp.bfloat16)
    sigmoid_scores = jax.nn.sigmoid(gate_scores)
    shares = sigmoid_scores / jnp.sum(sigmoid_scores, axis=-1, keepdims=True)
    one_hot = (
        expert_ids[:, :, None] == jnp.arange(EXPERTS, dtype=jnp.int32)[None, None, :]
    ).astype(jnp.float32)
    expert_weight = jnp.sum(shares[:, :, None] * one_hot, axis=1).astype(jnp.bfloat16)
    block = lax.all_gather(normed, "dev", axis=0, tiled=True)
    gate_act = jnp.dot(block, gate_weight, preferred_element_type=jnp.float32)
    up_act = jnp.dot(block, up_weight, preferred_element_type=jnp.float32)
    hidden = (jax.nn.silu(gate_act) * up_act).astype(jnp.bfloat16)
    at_owner = lax.all_to_all(hidden, "dev", split_axis=0, concat_axis=1, tiled=True)
    unit_blocks = jnp.transpose(
        at_owner.reshape(rows_here, splits, at_owner.shape[1] // splits), (1, 0, 2)
    )
    sending = jnp.repeat(unit_blocks, COLS, axis=0)
    arrived = lax.all_to_all(sending, "dev", split_axis=0, concat_axis=0, tiled=True)
    block_hidden = arrived.reshape(devices * rows_here, arrived.shape[2])
    expert_part = jnp.dot(block_hidden, down_weight[0], preferred_element_type=jnp.float32)
    returned_experts = lax.all_to_all(
        expert_part.reshape(devices, rows_here, expert_part.shape[1]).astype(jnp.bfloat16),
        "dev",
        split_axis=0,
        concat_axis=0,
        tiled=True,
    ).astype(jnp.float32)
    block_weight = jnp.repeat(jnp.transpose(expert_weight.astype(jnp.float32)), blocks_each, axis=0)
    mixture = fold_blocks(returned_experts, splits, rows_here, block_weight)
    return (attended + mixture).astype(jnp.bfloat16)


def solution(mesh):
    return jax.shard_map(
        body,
        mesh=mesh,
        in_specs=(
            P(("group", "dev"), None),
            P(("group", "dev"), None, None),
            P(("group", "dev"), None, None),
            P(("group", "dev")),
            P(("group", "dev"), None),
            P("dev", None, None),
            P(),
            P(("group", "dev"), None),
            P(("group", "dev"), None),
            P(None, "dev"),
            P(None, "dev"),
            P("dev", None, None),
        ),
        out_specs=P(("group", "dev"), None),
        check_vma=False,
    )
```

profile of v0, /device:TPU:0, one launch (start us, length us, event | category | flops | bytes accessed | tf_op | source)
XLA Modules:
  0.0 111.9 jit_solution(13288832067696337943)
XLA Ops:
  0.0 0.0 copy-start
  0.0 0.0 copy-start.1
  0.0 0.0 copy-start.2
  0.0 0.8 iota_compare_fusion
  0.8 0.4 copy-done
  1.2 1.1 %fusion.14 = f32[4,16,512]{2,1,0:T(8,128)S(1)} fusion(bf16[4,512,256]{2,1,0:T(8,128)(2,1)S(1)} %copy-done, pred[4,512]{1,0:T(4,128)(4,1)S(1)} %iota_compare_fusion, bf16[1,4,16,256]{3,1,2,0:T(4,128)(2,1)} %bitcast.55), kind=kOutput, calls=%fused_computation.12 | convolution fusion | flops 16842752 | bytes 1214464 | tf_op jit(solution)/shard_map/rhc,rlc->rhl/dot_general | solution.py:40
  2.4 0.2 fusion.25
  2.6 1.5 %convolution_convert_fusion = bf16[4,16,256]{2,1,0:T(8,128)(2,1)S(1)} fusion(bf16[4,512,256]{2,1,0:T(8,128)(2,1)} %param.14, f32[4,16]{1,0:T(4,128)S(1)} %fusion.25, f32[4,16,512]{2,1,0:T(8,128)S(1)} %fusion.14, pred[4,512]{1,0:T(4,128)(4,1)S(1)} %iota_compare_fusion), kind=kOutput, calls=%fused_computation.14 | convolution fusion | flops 16925248 | bytes 1214720 | tf_op jit(solution)/shard_map/rhl,rlc->rhc/dot_general | solution.py:49
  4.2 15.1 %all_to_all.36 = bf16[16,4,1024]{2,1,0:T(4,128)(2,1)S(1)} all-to-all(bf16[16,4,1024]{2,1,0:T(4,128)(2,1)S(1)} %bitcast.50), channel_id=1, replica_groups=mesh['group'=2,'dev'=16] {'dev'}, dimensions={0} | all-to-all | bytes 262144 | tf_op jit(solution)/shard_map/all_to_all | solution.py:56
  19.3 2.8 %fusion.5 = bf16[16,4,1792]{2,0,1:T(8,128)(2,1)S(1)} fusion(bf16[1,1024,1792]{2,1,0:T(8,128)(2,1)} %param.17, bf16[16,4,1024]{2,1,0:T(4,128)(2,1)S(1)} %all_to_all.36), kind=kOutput, calls=%fused_computation.5 | convolution fusion | flops 234995712 | bytes 4030464 | tf_op jit(solution)/shard_map/dot_general | solution.py:58
  22.1 0.1 copy.30
  22.3 12.1 %all_to_all.37 = bf16[16,4,1792]{2,1,0:T(4,128)(2,1)S(1)} all-to-all(bf16[16,4,1792]{2,1,0:T(4,128)(2,1)S(1)} %copy.30), channel_id=1, replica_groups=mesh['group'=2,'dev'=16] {'dev'}, dimensions={0} | all-to-all | bytes 458752 | tf_op jit(solution)/shard_map/all_to_all | solution.py:59
  34.4 0.1 convert_reduce_fusion
  34.5 0.0 copy-done.1
  34.5 0.2 multiply_reduce_fusion
  34.7 0.0 copy-done.2
  34.7 0.1 fusion.20
  34.8 22.4 %all-gather = bf16[16,4,7168]{2,1,0:T(4,128)(2,1)} all-gather(bf16[1,4,7168]{2,1,0:T(4,128)(2,1)S(1)} %fusion.20), channel_id=1, replica_groups=mesh['group'=2,'dev'=16] {'dev'}, dimensions={0}, use_global_device_ids=true | all-gather | bytes 974848 | tf_op jit(solution)/shard_map/all_gather | solution.py:75
  57.2 0.0 slice-start
  57.2 1.7 %reshape.93 = bf16[64,7168]{1,0:T(8,128)(2,1)S(1)} reshape(bf16[16,4,7168]{2,1,0:T(4,128)(2,1)} %all-gather) | data formatting | bytes 1835008
  58.9 0.0 slice-start.1
  58.9 0.0 slice-start.2
  59.0 5.3 %fusion.26 = f32[64,640]{1,0:T(8,128)S(1)} fusion(bf16[64,7168]{1,0:T(8,128)(2,1)S(1)} %reshape.93, bf16[7168,640]{1,0:T(8,128)(2,1)} %param.21), kind=kOutput, calls=%fused_computation.40 | convolution fusion | flops 587202560 | bytes 10256384 | tf_op jit(solution)/shard_map/dot_general | solution.py:76
  64.3 0.0 slice-done
  64.3 0.0 slice-done.1
  64.3 0.7 slice-done.2
  65.0 0.0 copy-start.3
  65.0 1.6 %fusion.15 = bf16[64,640]{1,0:T(8,128)(2,1)S(1)} fusion(bf16[64,7168]{1,0:T(8,128)(2,1)S(1)} %reshape.93, bf16[7168,640]{1,0:T(8,128)(2,1)S(1)} %bitcast.44, f32[64,640]{1,0:T(8,128)S(1)} %fusion.26), kind=kOutput, calls=%fused_computation.13 | convolution fusion | flops 587448320 | bytes 10338304 | tf_op jit(solution)/shard_map/dot_general | solution.py:77
  66.7 0.0 copy-start.4
  66.7 9.7 %all_to_all.38 = bf16[16,4,640]{2,1,0:T(4,128)(2,1)S(1)} all-to-all(bf16[16,4,640]{2,1,0:T(4,128)(2,1)S(1)} %all_to_all.26), channel_id=1, replica_groups=mesh['group'=2,'dev'=16] {'dev'}, dimensions={0} | all-to-all | bytes 163840 | tf_op jit(solution)/shard_map/all_to_all | solution.py:79
  76.5 0.8 broadcast_in_dim.39
  77.3 3.5 %all-to-all-start.3 = ((bf16[16,4,2560]{2,1,0:T(4,128)(2,1)}), bf16[16,4,2560]{2,1,0:T(4,128)(2,1)S(1)}, u32[]{:S(2)}, u32[]{:S(2)}) async-start(bf16[16,4,2560]{2,1,0:T(4,128)(2,1)} %bitcast.10), calls=%async_computation.3 | async-start | bytes 655360 | tf_op jit(solution)/shard_map/all_to_all | solution.py:84
  80.9 0.0 copy-done.3
  80.9 0.1 divide_reduce_fusion
  81.0 10.9 %all-to-all-done.3 = bf16[16,4,2560]{2,1,0:T(4,128)(2,1)S(1)} async-done(((bf16[16,4,2560]{2,1,0:T(4,128)(2,1)}), bf16[16,4,2560]{2,1,0:T(4,128)(2,1)S(1)}, u32[]{:S(2)}, u32[]{:S(2)}) %all-to-all-start.3) | async-done | bytes 327712 | tf_op jit(solution)/shard_map/all_to_all | solution.py:84
  91.9 5.3 %fusion.8 = bf16[16,4,1792]{2,0,1:T(8,128)(2,1)S(1)} fusion(bf16[1,2560,1792]{2,1,0:T(8,128)(2,1)} %param.23, bf16[16,4,2560]{2,1,0:T(4,128)(2,1)S(1)} %all-to-all-done.3), kind=kOutput, calls=%fused_computation.6 | convolution fusion | flops 587317248 | bytes 9732096 | tf_op jit(solution)/shard_map/dot_general | solution.py:86
  97.2 0.8 copy.34
  98.0 3.5 %all-to-all-start.4 = ((bf16[16,4,1792]{2,1,0:T(4,128)(2,1)}), bf16[16,4,1792]{2,1,0:T(4,128)(2,1)S(1)}, u32[]{:S(2)}, u32[]{:S(2)}) async-start(bf16[16,4,1792]{2,1,0:T(4,128)(2,1)} %copy.34), calls=%async_computation.4 | async-start | bytes 458752 | tf_op jit(solution)/shard_map/all_to_all | solution.py:87
  101.6 0.1 multiply_divide_fusion
  101.6 0.1 copy.36
  101.7 0.0 copy-done.4
  101.7 0.1 copy.35
  101.8 0.1 select_reduce_fusion
  101.9 0.1 copy.37
  102.0 9.0 %all-to-all-done.4 = bf16[16,4,1792]{2,1,0:T(4,128)(2,1)S(1)} async-done(((bf16[16,4,1792]{2,1,0:T(4,128)(2,1)}), bf16[16,4,1792]{2,1,0:T(4,128)(2,1)S(1)}, u32[]{:S(2)}, u32[]{:S(2)}) %all-to-all-start.4) | async-done | bytes 229408 | tf_op jit(solution)/shard_map/all_to_all | solution.py:87
  111.1 0.2 fusion.16
  111.3 0.7 add_convert_fusion
  (10 shorter events, 0.2 us)
Async XLA Ops:
  0.0 1.2 %copy-start = (bf16[4,512,256]{2,1,0:T(8,128)(2,1)S(1)}, bf16[4,512,256]{2,1,0:T(8,128)(2,1)}, u32[]{:S(2)}) copy-start(bf16[4,512,256]{2,1,0:T(8,128)(2,1)} %param.13) | copy-start | bytes 3145732
  0.0 34.5 %copy-start.1 = (bf16[4,7168]{1,0:T(4,128)(2,1)S(1)}, bf16[4,7168]{1,0:T(4,128)(2,1)}, u32[]{:S(2)}) copy-start(bf16[4,7168]{1,0:T(4,128)(2,1)} %param.16) | copy-start | bytes 172036
  0.0 34.7 %copy-start.2 = (f32[7168]{0:T(1024)S(1)}, f32[7168]{0:T(1024)}, u32[]{:S(2)}) copy-start(f32[7168]{0:T(1024)} %param.18) | copy-start | bytes 86020
  57.2 7.1 %slice-start = ((s8[9175040]{0:T(1024)(128)(4,1)}), s8[786432]{0:T(1024)(128)(4,1)S(1)}, s32[]{:S(2)}) async-start(s8[9175040]{0:T(1024)(128)(4,1)} %bitcast.43), calls=%async_computation.5 | async-start | bytes 1572864
  58.9 5.4 %slice-start.1 = ((s8[9175040]{0:T(1024)(128)(4,1)}), s8[4194304]{0:T(1024)(128)(4,1)S(1)}, s32[]{:S(2)}) async-start(s8[9175040]{0:T(1024)(128)(4,1)} %bitcast.43), calls=%async_computation.6 | async-start | bytes 8388608
  58.9 6.1 %slice-start.2 = ((s8[9175040]{0:T(1024)(128)(4,1)}), s8[4194304]{0:T(1024)(128)(4,1)S(1)}, s32[]{:S(2)}) async-start(s8[9175040]{0:T(1024)(128)(4,1)} %bitcast.43), calls=%async_computation.7 | async-start | bytes 8388608
  65.0 15.9 %copy-start.3 = (f32[4,3]{1,0:T(4,128)S(1)}, f32[4,3]{1,0:T(4,128)}, u32[]{:S(2)}) copy-start(f32[4,3]{1,0:T(4,128)} %param.20) | copy-start | bytes 148
  66.7 35.1 %copy-start.4 = (s32[4,3]{1,0:T(4,128)S(1)}, s32[4,3]{1,0:T(4,128)}, u32[]{:S(2)}) copy-start(s32[4,3]{1,0:T(4,128)} %param.19) | copy-start | bytes 148
  77.3 14.6 %all-to-all-start.3 = ((bf16[16,4,2560]{2,1,0:T(4,128)(2,1)}), bf16[16,4,2560]{2,1,0:T(4,128)(2,1)S(1)}, u32[]{:S(2)}, u32[]{:S(2)}) async-start(bf16[16,4,2560]{2,1,0:T(4,128)(2,1)} %bitcast.10), calls=%async_computation.3 | async-start | bytes 655360 | tf_op jit(solution)/shard_map/all_to_all | solution.py:84
  98.0 13.0 %all-to-all-start.4 = ((bf16[16,4,1792]{2,1,0:T(4,128)(2,1)}), bf16[16,4,1792]{2,1,0:T(4,128)(2,1)S(1)}, u32[]{:S(2)}, u32[]{:S(2)}) async-start(bf16[16,4,1792]{2,1,0:T(4,128)(2,1)} %copy.34), calls=%async_computation.4 | async-start | bytes 458752 | tf_op jit(solution)/shard_map/all_to_all | solution.py:87
where the time goes:
time: 113 us; the launch traced here: 112 us
  blocking collectives  59.4 us (53%)
  waiting for transfers between devices  20 us (18%)
  matrix products  17.8 us (16%)
  starting transfers between devices  7.07 us (6%)
  local copies, waits for them, and re-layouts  5.06 us (4%)
  other arithmetic  2.57 us (2%)
    all_gather x1, blocking collectives, body(): block = lax.all_gather(normed, 'dev', axis=0, tiled=True)  22.4 us
    all_to_all x1, blocking collectives, body(): lax.all_to_all(outgoing, 'dev', split_axis=0, concat_axis=0, tiled=True)  15.1 us
    all_to_all x1, blocking collectives, body(): lax.all_to_all(head_part.reshape(devices, rows_here, head_part.shape[1])....  12.1 us
    all_to_all x1, waiting for transfers between devices, body(): lax.all_to_all(sending, 'dev', split_axis=0, concat_axis=0, tiled=True)  10.9 us
    all_to_all x1, blocking collectives, body(): lax.all_to_all(hidden, 'dev', split_axis=0, concat_axis=1, tiled=True)  9.73 us
    all_to_all x1, waiting for transfers between devices, body(): lax.all_to_all(expert_part.reshape(devices, rows_here, expert_part.shape[...  9.03 us
    dot_general x1, matrix products, body(): gate_act = jnp.dot(block, gate_weight, preferred_element_type=jnp.float32)  5.34 us
    dot_general x1, matrix products, body(): jnp.dot(block_hidden, down_weight[0], preferred_element_type=jnp.float32)  5.3 us
  transfers between devices with their start and end apart: 2, of which 2 were waited for; matrix products, arithmetic and copies ran while one was open for 0% of the time, Pallas kernels for 0%

commit v1 on v0

v1 whole, which is shorter than its diff:
```python
import functools

import jax
import jax.numpy as jnp
from jax import lax
from jax.experimental import pallas as pl
from jax.experimental.pallas import tpu as pltpu
from jax.sharding import PartitionSpec as P

EXPERTS = 4
COLS = 4
LANES = 128
F32 = jnp.float32
BF16 = jnp.bfloat16


def dot(a, b):
    return jnp.dot(a, b, preferred_element_type=F32)


def kernel(
    n,
    q_ref,
    len_ref,
    res_ref,
    gain_ref,
    ids_ref,
    score_ref,
    keys_hbm,
    values_hbm,
    wo_hbm,
    wg_hbm,
    wu_hbm,
    wd_hbm,
    out_ref,
    keys,
    values,
    wo,
    wg,
    wu,
    wd,
    q_rows,
    ctx_send,
    ctx_recv,
    ctx_all,
    mix_send,
    mix_recv,
    mix_all,
    res_recv,
    part,
    part_send,
    part_recv,
    attended,
    y_all,
    hid_all,
    acc,
    fin_send,
    fin_recv,
    kv_sem,
    w_sem,
    ctx_ssem,
    ctx_rsem,
    mix_ssem,
    mix_rsem,
    res_ssem,
    res_rsem,
    part_ssem,
    part_rsem,
    z_ssem,
    z_rsem,
    y_ssem,
    y_rsem,
    c_ssem,
    c_rsem,
    hid_ssem,
    hid_rsem,
    fin_ssem,
    fin_rsem,
):
    me = lax.axis_index("dev")
    splits = n // COLS
    k = me // COLS
    c = lax.rem(me, COLS)
    rows = q_ref.shape[0]
    head_dim = keys.shape[2]
    cache_len = keys.shape[1]
    heads = q_ref.shape[1] // head_dim
    per_block = heads // splits
    kb = wo.shape[0]
    db = wo.shape[1]
    ff = wg.shape[1]
    blk = rows * COLS
    all_rows = rows * n
    width = db * COLS

    def remote(src, dst, ssem, rsem, dev):
        return pltpu.make_async_remote_copy(
            src_ref=src,
            dst_ref=dst,
            send_sem=ssem,
            recv_sem=rsem,
            device_id={"dev": dev},
            device_id_type=pl.DeviceIdType.MESH,
        )

    loads = []
    for r in range(rows):
        loads.append(pltpu.make_async_copy(keys_hbm.at[r], keys.at[r], kv_sem.at[r]))
    for r in range(rows):
        loads.append(pltpu.make_async_copy(values_hbm.at[r], values.at[r], kv_sem.at[rows + r]))
    for copy in loads:
        copy.start()
    load_o = pltpu.make_async_copy(wo_hbm.at[0], wo, w_sem.at[0])

    def xor(a, bit):
        return a + bit - 2 * bit * lax.rem(a // bit, 2)

    beside = xor(c, 1)
    across = xor(c, 2)
    corner = xor(beside, 2)

    def plane(i):
        return (c, beside, across, corner)[i]

    def w_slice(i):
        return pl.ds(pl.multiple_of(plane(i) * db, db), db)

    load_g = [
        pltpu.make_async_copy(wg_hbm.at[w_slice(i)], wg.at[w_slice(i)], w_sem.at[1 + i])
        for i in range(COLS)
    ]
    load_u = [
        pltpu.make_async_copy(wu_hbm.at[w_slice(i)], wu.at[w_slice(i)], w_sem.at[5 + i])
        for i in range(COLS)
    ]

    def d_slice(i):
        return pl.ds(pl.multiple_of(plane(i) * ff, ff), ff)

    load_d = [
        pltpu.make_async_copy(wd_hbm.at[0, d_slice(i)], wd.at[d_slice(i)], w_sem.at[9 + i])
        for i in range(COLS)
    ]

    barrier = pltpu.get_barrier_semaphore()

    def greet(i, carry):
        pl.semaphore_signal(
            barrier,
            inc=1,
            device_id={"dev": lax.rem(me + i, n)},
            device_id_type=pl.DeviceIdType.MESH,
        )
        return carry

    lax.fori_loop(1, n, greet, 0)
    load_o.start()
    for i in range(COLS):
        load_g[i].start()
        load_u[i].start()
    for i in range(COLS):
        load_d[i].start()

    shares = 1.0 / (1.0 + jnp.exp(-score_ref[...]))
    total = jnp.sum(shares, axis=-1, keepdims=True)
    lane = lax.broadcasted_iota(jnp.int32, (rows, LANES), 1)
    mine = jnp.zeros((rows, LANES), F32)
    for t in range(ids_ref.shape[1]):
        share = shares[:, t : t + 1] / total
        mine = mine + jnp.where(ids_ref[:, t : t + 1] == lane, share, 0.0)
    mix_send[...] = mine.astype(BF16).astype(F32)

    for h in range(heads):
        q_rows[h * rows : (h + 1) * rows, :] = q_ref[:, h * head_dim : (h + 1) * head_dim].astype(
            F32
        )
    qs = q_rows[...].astype(BF16)
    hr = heads * rows
    which = lax.rem(lax.broadcasted_iota(jnp.int32, (hr, 1), 0), rows)
    scores = jnp.zeros((hr, cache_len), F32)
    lengths = jnp.zeros((hr, 1), jnp.int32)
    for r in range(rows):
        loads[r].wait()
        s = lax.dot_general(qs, keys[r], (((1,), (1,)), ((), ())), preferred_element_type=F32)
        scores = jnp.where(which == r, s, scores)
        lengths = jnp.where(which == r, len_ref[r], lengths)
    live = lax.broadcasted_iota(jnp.int32, (hr, cache_len), 1) < lengths
    scores = jnp.where(live, scores * head_dim ** (-0.5), -1e30)
    largest = jnp.max(scores, axis=-1, keepdims=True)
    exponent = jnp.where(live, jnp.exp(scores - largest), 0.0)
    probs = exponent / jnp.sum(exponent, axis=-1, keepdims=True)
    context = jnp.zeros((hr, head_dim), F32)
    for r in range(rows):
        loads[rows + r].wait()
        context = context + dot(jnp.where(which == r, probs, 0.0).astype(BF16), values[r])
    for h in range(heads):
        b, at = h // per_block, h % per_block
        ctx_send[b, :, at * head_dim : (at + 1) * head_dim] = context[
            h * rows : (h + 1) * rows, :
        ].astype(BF16)

    pl.semaphore_wait(barrier, n - 1)

    def ctx_copy(i):
        to = lax.rem(me + i, n)
        return remote(
            ctx_send.at[to // COLS], ctx_recv.at[me], ctx_ssem.at[i], ctx_rsem.at[i], to
        )

    def mix_copy(i):
        to = lax.rem(me + i, n)
        return remote(mix_send, mix_recv.at[me], mix_ssem.at[i], mix_rsem.at[i], to)

    def res_copy(i):
        to = lax.rem(c + i, COLS)
        cols = pl.ds(pl.multiple_of(to * db, LANES), db)
        return remote(
            res_ref.at[:, cols], res_recv.at[c], res_ssem.at[i], res_rsem.at[i], k * COLS + to
        )

    def loop(low, high, f):
        def step(i, carry):
            f(i)
            return carry

        lax.fori_loop(low, high, step, 0)

    loop(1, n, lambda i: ctx_copy(i).start())
    loop(1, COLS, lambda i: res_copy(i).start())
    loop(1, n, lambda i: mix_copy(i).start())
    ctx_recv[me] = ctx_send[k]
    mix_recv[me] = mix_send[...]
    res_recv[c] = res_ref[:, pl.ds(pl.multiple_of(c * db, LANES), db)]
    load_o.wait()
    loop(1, n, lambda i: ctx_copy(i).wait_recv())
    for d in range(n):
        ctx_all[d * rows : (d + 1) * rows, :] = ctx_recv[d].astype(F32)
    part[...] = dot(ctx_all[...].astype(BF16), wo[...])

    for b in range(splits):
        part_send[b] = part[b * blk : (b + 1) * blk, :].astype(BF16)

    def part_copy(i):
        to = lax.rem(k + i, splits)
        return remote(
            part_send.at[to], part_recv.at[i], part_ssem.at[i], part_rsem.at[i], to * COLS + c
        )

    loop(1, splits, lambda i: part_copy(i).start())
    loop(1, COLS, lambda i: res_copy(i).wait_recv())
    for j in range(COLS):
        attended[j * rows : (j + 1) * rows, :] = res_recv[j].astype(F32)
    mine_rows = pl.ds(pl.multiple_of(k * blk, blk), blk)
    total = attended[...] + part[mine_rows, :]
    gain = gain_ref[:, pl.ds(pl.multiple_of(c * db, LANES), db)]
    for i in range(1, splits):
        part_copy(i).wait_recv()
        total = total + part_recv[i].astype(F32)
    attended[...] = total
    square = jnp.sum(total * total, axis=-1, keepdims=True)
    high = square.astype(BF16).astype(F32)
    lane = lax.broadcasted_iota(jnp.int32, (blk, LANES), 1)
    packed = jnp.where(lane == 0, high, jnp.where(lane == 1, square - high, 0.0))
    y_all[c, mine_rows, 0:db] = (total * gain).astype(BF16)
    y_all[c, mine_rows, db : db + LANES] = packed.astype(BF16)

    def piece(col, i):
        from_k = lax.rem(k + splits - i, splits)
        return y_all.at[col, pl.ds(pl.multiple_of(from_k * blk, blk), blk)]

    def z_copy(i):
        to = lax.rem(k + i, splits)
        return remote(piece(c, 0), piece(c, 0), z_ssem.at[i], z_rsem.at[i], to * COLS + c)

    def y_copy(i):
        return remote(
            piece(c, i), piece(c, i), y_ssem.at[i], y_rsem.at[i], k * COLS + across
        )

    def c_copy(col, base, i):
        return remote(
            piece(col, i),
            piece(col, i),
            c_ssem.at[base + i],
            c_rsem.at[base + i],
            k * COLS + beside,
        )

    loop(1, splits, lambda i: z_copy(i).start())
    y_copy(0).start()
    c_copy(c, 0, 0).start()

    def forward_z(i):
        z_copy(i).wait_recv()
        y_copy(i).start()
        c_copy(c, 0, i).start()

    def forward_y(i):
        y_copy(i).wait_recv()
        c_copy(across, splits, i).start()

    loop(1, splits, forward_z)

    def chunk(i, col):
        load_g[i].wait()
        load_u[i].wait()
        lhs = y_all[col, :, 0:db]
        at = pl.ds(pl.multiple_of(col * db, db), db)
        tail = y_all[col, :, db : db + LANES].astype(F32)
        return dot(lhs, wg[at, :]), dot(lhs, wu[at, :]), jnp.sum(tail, axis=-1, keepdims=True)

    gate, up, square = chunk(0, c)
    loop(0, splits, forward_y)
    loop(0, splits, lambda i: c_copy(beside, 0, i).wait_recv())
    g, u, s = chunk(1, beside)
    gate, up, square = gate + g, up + u, square + s
    g, u, s = chunk(2, across)
    gate, up, square = gate + g, up + u, square + s
    loop(0, splits, lambda i: c_copy(corner, splits, i).wait_recv())
    g, u, s = chunk(3, corner)
    gate, up, square = gate + g, up + u, square + s
    scale = lax.rsqrt(square * (1.0 / width) + 1e-5)
    gate = gate * scale
    hidden = gate / (1.0 + jnp.exp(-gate)) * (up * scale)
    hid_all[c] = hidden.astype(BF16)

    def hid_copy(i):
        return remote(
            hid_all.at[c], hid_all.at[c], hid_ssem.at[i], hid_rsem.at[i], k * COLS + plane(i)
        )

    for i in (2, 3, 1):
        hid_copy(i).start()
    loop(1, n, lambda i: mix_copy(i).wait_recv())
    for d in range(n):
        mix_all[d * rows : (d + 1) * rows, :] = mix_recv[d]
    lane = lax.broadcasted_iota(jnp.int32, (all_rows, LANES), 1)
    expert = k // (splits // EXPERTS)
    weight = jnp.sum(jnp.where(lane == expert, mix_all[...], 0.0), axis=-1, keepdims=True)
    for i in range(COLS):
        load_d[i].wait()
        if i:
            hid_copy(i).wait_recv()
        at = pl.ds(pl.multiple_of(plane(i) * ff, ff), ff)
        term = dot(hid_all[plane(i)], wd[at, :])
        acc[...] = term if i == 0 else acc[...] + term
    acc[...] = acc[...] * weight
    acc[mine_rows, :] = acc[mine_rows, :] + attended[...]
    for d in range(n):
        fin_send[d] = acc[d * rows : (d + 1) * rows, :].astype(BF16)

    def fin_copy(i):
        to = lax.rem(me + i, n)
        return remote(fin_send.at[to], fin_recv.at[me], fin_ssem.at[i], fin_rsem.at[i], to)

    loop(1, n, lambda i: fin_copy(i).start())
    fin_recv[me] = fin_send[me]
    loop(1, n, lambda i: fin_copy(i).wait_recv())
    for j in range(COLS):
        total = fin_recv[j].astype(F32)
        for b in range(1, splits):
            total = total + fin_recv[b * COLS + j].astype(F32)
        out_ref[:, j * db : (j + 1) * db] = total.astype(BF16)

    def drain(i):
        ctx_copy(i).wait_send()
        mix_copy(i).wait_send()
        fin_copy(i).wait_send()

    loop(1, n, drain)

    def drain_split(i):
        part_copy(i).wait_send()
        z_copy(i).wait_send()

    loop(1, splits, drain_split)

    def drain_plane(i):
        y_copy(i).wait_send()
        c_copy(c, 0, i).wait_send()
        c_copy(across, splits, i).wait_send()

    loop(0, splits, drain_plane)
    for i in range(1, COLS):
        res_copy(i).wait_send()
        hid_copy(i).wait_send()


def body(
    queries,
    cache_keys,
    cache_values,
    row_lengths,
    residual,
    out_weight,
    norm_gain,
    expert_ids,
    gate_scores,
    gate_weight,
    up_weight,
    down_weight,
):
    n = lax.axis_size("dev")
    splits = n // COLS
    rows = queries.shape[0]
    head_dim = cache_keys.shape[2]
    heads = queries.shape[1] // head_dim
    kb, db = out_weight.shape[1:]
    ff = gate_weight.shape[1]
    all_rows = rows * n
    blk = rows * COLS
    vmem = pl.BlockSpec(memory_space=pltpu.VMEM)
    hbm = pl.BlockSpec(memory_space=pl.ANY)
    smem = pl.BlockSpec(memory_space=pltpu.SMEM)

    def dma(*count):
        return pltpu.SemaphoreType.DMA(count)

    return pl.pallas_call(
        functools.partial(kernel, n),
        out_shape=jax.ShapeDtypeStruct(residual.shape, BF16),
        in_specs=[vmem, smem, vmem, vmem, vmem, vmem] + [hbm] * 6,
        out_specs=vmem,
        scratch_shapes=[
            pltpu.VMEM(cache_keys.shape, BF16),
            pltpu.VMEM(cache_values.shape, BF16),
            pltpu.VMEM((kb, db), BF16),
            pltpu.VMEM(gate_weight.shape, BF16),
            pltpu.VMEM(up_weight.shape, BF16),
            pltpu.VMEM(down_weight.shape[1:], BF16),
            pltpu.VMEM((heads * rows, head_dim), F32),
            pltpu.VMEM((splits, rows, kb), BF16),
            pltpu.VMEM((n, rows, kb), BF16),
            pltpu.VMEM((all_rows, kb), F32),
            pltpu.VMEM((rows, LANES), F32),
            pltpu.VMEM((n, rows, LANES), F32),
            pltpu.VMEM((all_rows, LANES), F32),
            pltpu.VMEM((COLS, rows, db), BF16),
            pltpu.VMEM((all_rows, db), F32),
            pltpu.VMEM((splits, blk, db), BF16),
            pltpu.VMEM((splits, blk, db), BF16),
            pltpu.VMEM((blk, db), F32),
            pltpu.VMEM((COLS, all_rows, db + LANES), BF16),
            pltpu.VMEM((COLS, all_rows, ff), BF16),
            pltpu.VMEM((all_rows, db), F32),
            pltpu.VMEM((n, rows, db), BF16),
            pltpu.VMEM((n, rows, db), BF16),
            dma(2 * rows),
            dma(13),
            dma(n),
            dma(n),
            dma(n),
            dma(n),
            dma(COLS),
            dma(COLS),
            dma(splits),
            dma(splits),
            dma(splits),
            dma(splits),
            dma(splits),
            dma(splits),
            dma(2 * splits),
            dma(2 * splits),
            dma(COLS),
            dma(COLS),
            dma(n),
            dma(n),
        ],
        compiler_params=pltpu.CompilerParams(
            collective_id=0, has_side_effects=True, vmem_limit_bytes=60 * 1024 * 1024
        ),
        name="layer",
    )(
        queries,
        row_lengths,
        residual,
        norm_gain[None, :],
        expert_ids,
        gate_scores,
        cache_keys,
        cache_values,
        out_weight,
        gate_weight,
        up_weight,
        down_weight,
    )


def solution(mesh):
    return jax.shard_map(
        body,
        mesh=mesh,
        in_specs=(
            P(("group", "dev"), None),
            P(("group", "dev"), None, None),
            P(("group", "dev"), None, None),
            P(("group", "dev")),
            P(("group", "dev"), None),
            P("dev", None, None),
            P(),
            P(("group", "dev"), None),
            P(("group", "dev"), None),
            P(None, "dev"),
            P(None, "dev"),
            P("dev", None, None),
        ),
        out_specs=P(("group", "dev"), None),
        check_vma=False,
    )
```

time: 113 us -> 47 us (0.42)
  blocking collectives: 59.4 us -> 0 us
  Pallas kernels: 0 us -> 44.9 us
  waiting for transfers between devices: 20 us -> 0 us
  matrix products: 17.8 us -> 0 us
  starting transfers between devices: 7.07 us -> 0 us
  local copies, waits for them, and re-layouts: 5.06 us -> 1.46 us
  other arithmetic: 2.57 us -> 0 us
    pallas_call x0 -> x1, Pallas kernels: none -> 44.9 us  [body(): pl.pallas_call(functools.partial(kernel, n), out_shape=jax.ShapeDtypeStru...]
    all_to_all x3 -> x0, blocking collectives: 37 us -> none  [the longest x1 15.1 us: body(): lax.all_to_all(outgoing, 'dev', split_axis=0, concat_axis=0, tiled=True)]
    all_gather x1 -> x0, blocking collectives: 22.4 us -> none  [body(): block = lax.all_gather(normed, 'dev', axis=0, tiled=True)]
    all_to_all x2 -> x0, waiting for transfers between devices: 20 us -> none  [the longest x1 10.9 us: body(): lax.all_to_all(sending, 'dev', split_axis=0, concat_axis=0, tiled=True)]
    dot_general x6 -> x0, matrix products: 17.8 us -> none  [the longest x1 5.34 us: body(): gate_act = jnp.dot(block, gate_weight, preferred_element_type=jnp.float32)]
    all_to_all x2 -> x0, starting transfers between devices: 7.07 us -> none  [the longest x1 3.54 us: body(): lax.all_to_all(sending, 'dev', split_axis=0, concat_axis=0, tiled=True)]
    unnamed x18 -> x1, local copies, waits for them, and re-layouts: 2.96 us -> 1.46 us
  transfers between devices with their start and end apart: 2 -> 0, of which waited for: 2 -> 0; matrix products, arithmetic and copies ran while one was open for 0% -> 0% of each run, Pallas kernels for 0% -> 0%
where the time goes in v1:
time: 47 us; the launch traced here: 46.3 us
  Pallas kernels  44.9 us (96%)
  local copies, waits for them, and re-layouts  1.46 us (3%)
    pallas_call x1, Pallas kernels, body(): pl.pallas_call(functools.partial(kernel, n), out_shape=jax.ShapeDtypeStru...  44.9 us
    unnamed x1, local copies, waits for them, and re-layouts  1.46 us

profile of v1, /device:TPU:0, one launch (start us, length us, event | category | flops | bytes accessed | tf_op | source)
XLA Modules:
  0.0 46.3 jit_solution(10718681655116414261)
XLA Ops:
  0.0 44.9 %layer.1 = bf16[4,7168]{1,0:T(4,128)(2,1)} custom-call(bf16[4,4096]{1,0:T(4,128)(2,1)} %q_ref.1, s32[4]{0:T(128)} %len_ref.1, bf16[4,7168]{1,0:T(4,128)(2,1)} %res_ref.1, f32[1,7168]{1,0:T(1,128)} %bitcast.1, s32[4,3]{1,0:T(4,128)} %ids_ref.1, f32[4,3]{1,0:T(4,128)} %score_ref.1, bf16[4,512,256]{2,1,0:T(8,128)(2,1)} %keys_hbm.1, ...), custom_call_target="tpu_custom_call" | custom-call | tf_op jit(solution)/shard_map/layer/pallas_call | solution.py:419
  44.9 1.5 %copy.14 = bf16[4,7168]{1,0:T(4,128)(2,1)} copy(bf16[4,7168]{1,0:T(4,128)(2,1)} %layer.1) | data formatting | bytes 114688

commit v2 on v1

v2 whole, which is shorter than its diff:
```python
import functools

import jax
import jax.numpy as jnp
from jax import lax
from jax.experimental import pallas as pl
from jax.experimental.pallas import tpu as pltpu
from jax.sharding import PartitionSpec as P

EXPERTS = 4
COLS = 4
LANES = 128
HALVES = 2
F32 = jnp.float32
BF16 = jnp.bfloat16


def dot(a, b):
    return jnp.dot(a, b, preferred_element_type=F32)


def kernel(
    n,
    q_hbm,
    len_hbm,
    res_hbm,
    gain_hbm,
    ids_hbm,
    score_hbm,
    keys_hbm,
    values_hbm,
    wo_hbm,
    wg_hbm,
    wu_hbm,
    wd_hbm,
    out_ref,
    q_ref,
    len_ref,
    res_ref,
    gain_ref,
    ids_ref,
    score_ref,
    keys,
    values,
    wo,
    wg,
    wu,
    wd,
    q_rows,
    ctx_send,
    ctx_recv,
    ctx_all,
    res_send,
    res_recv,
    extra,
    part,
    part_send,
    part_recv,
    attended,
    y_first,
    y_second,
    hid_all,
    acc,
    fin_send,
    fin_recv,
    in_sem,
    kv_sem,
    w_sem,
    ctx_ssem,
    ctx_rsem,
    res_ssem,
    res_rsem,
    part_ssem,
    part_rsem,
    z_ssem,
    z_rsem,
    y_ssem,
    y_rsem,
    c_ssem,
    c_rsem,
    hid_ssem,
    hid_rsem,
    fin_ssem,
    fin_rsem,
):
    me = lax.axis_index("dev")
    splits = n // COLS
    k = me // COLS
    c = lax.rem(me, COLS)
    rows = q_ref.shape[0]
    head_dim = keys.shape[2]
    cache_len = keys.shape[1]
    heads = q_ref.shape[1] // head_dim
    per_block = heads // splits
    db = wo.shape[1]
    half = db // HALVES
    ff = wg.shape[1]
    blk = rows * COLS
    all_rows = rows * n
    width = db * COLS
    y_all = (y_first, y_second)

    barrier = pltpu.get_barrier_semaphore()

    def loop(low, high, f):
        def step(i, carry):
            f(i)
            return carry

        lax.fori_loop(low, high, step, 0)

    def greet(i):
        pl.semaphore_signal(
            barrier,
            inc=1,
            device_id={"dev": lax.rem(me + i, n)},
            device_id_type=pl.DeviceIdType.MESH,
        )

    loop(1, n, greet)

    def remote(src, dst, ssem, rsem, dev):
        return pltpu.make_async_remote_copy(
            src_ref=src,
            dst_ref=dst,
            send_sem=ssem,
            recv_sem=rsem,
            device_id={"dev": dev},
            device_id_type=pl.DeviceIdType.MESH,
        )

    def xor(a, bits):
        bit = 1
        while bit <= bits:
            if bits & bit:
                a = a + bit - 2 * bit * lax.rem(a // bit, 2)
            bit *= 2
        return a

    beside = xor(c, 1)
    across = xor(c, 2)
    corner = xor(c, 3)
    plane = (c, beside, across, corner)

    small = [
        pltpu.make_async_copy(src, dst, in_sem.at[i])
        for i, (src, dst) in enumerate(
            (
                (q_hbm, q_ref),
                (len_hbm, len_ref),
                (res_hbm, res_ref),
                (gain_hbm, gain_ref),
                (ids_hbm, ids_ref),
                (score_hbm, score_ref),
            )
        )
    ]
    loads = [pltpu.make_async_copy(keys_hbm.at[r], keys.at[r], kv_sem.at[r]) for r in range(rows)]
    loads += [
        pltpu.make_async_copy(values_hbm.at[r], values.at[r], kv_sem.at[rows + r])
        for r in range(rows)
    ]
    load_o = pltpu.make_async_copy(wo_hbm.at[0], wo, w_sem.at[0])

    def span(i, size):
        return pl.ds(pl.multiple_of(plane[i] * size, size), size)

    load_g = [
        pltpu.make_async_copy(wg_hbm.at[span(i, db)], wg.at[span(i, db)], w_sem.at[1 + i])
        for i in range(COLS)
    ]
    load_u = [
        pltpu.make_async_copy(wu_hbm.at[span(i, db)], wu.at[span(i, db)], w_sem.at[5 + i])
        for i in range(COLS)
    ]
    load_d = [
        pltpu.make_async_copy(wd_hbm.at[0, span(i, ff)], wd.at[span(i, ff)], w_sem.at[9 + i])
        for i in range(COLS)
    ]
    small[0].start()
    small[1].start()
    for copy in loads:
        copy.start()
    for copy in small[2:]:
        copy.start()
    load_o.start()
    for i in range(COLS):
        load_g[i].start()
        load_u[i].start()
    for i in range(COLS):
        load_d[i].start()

    small[0].wait()
    small[1].wait()
    for h in range(heads):
        q_rows[h * rows : (h + 1) * rows, :] = q_ref[:, h * head_dim : (h + 1) * head_dim].astype(
            F32
        )
    qs = q_rows[...].astype(BF16)
    hr = heads * rows
    which = lax.rem(lax.broadcasted_iota(jnp.int32, (hr, 1), 0), rows)
    scores = jnp.zeros((hr, cache_len), F32)
    lengths = jnp.zeros((hr, 1), jnp.int32)
    for r in range(rows):
        loads[r].wait()
        s = lax.dot_general(qs, keys[r], (((1,), (1,)), ((), ())), preferred_element_type=F32)
        scores = jnp.where(which == r, s, scores)
        lengths = jnp.where(which == r, len_ref[r], lengths)
    live = lax.broadcasted_iota(jnp.int32, (hr, cache_len), 1) < lengths
    scores = jnp.where(live, scores * head_dim ** (-0.5), -1e30)
    largest = jnp.max(scores, axis=-1, keepdims=True)
    exponent = jnp.where(live, jnp.exp(scores - largest), 0.0)
    probs = exponent / jnp.sum(exponent, axis=-1, keepdims=True)
    context = jnp.zeros((hr, head_dim), F32)
    for r in range(rows):
        loads[rows + r].wait()
        context = context + dot(jnp.where(which == r, probs, 0.0).astype(BF16), values[r])
    for h in range(heads):
        b, at = h // per_block, h % per_block
        ctx_send[b, :, at * head_dim : (at + 1) * head_dim] = context[
            h * rows : (h + 1) * rows, :
        ].astype(BF16)

    for copy in small[2:]:
        copy.wait()
    shares = 1.0 / (1.0 + jnp.exp(-score_ref[...]))
    total = jnp.sum(shares, axis=-1, keepdims=True)
    lane = lax.broadcasted_iota(jnp.int32, (rows, LANES), 1)
    mine = jnp.zeros((rows, LANES), F32)
    for t in range(ids_ref.shape[1]):
        share = shares[:, t : t + 1] / total
        mine = mine + jnp.where(ids_ref[:, t : t + 1] + 2 == lane, share, 0.0)
    for j in range(COLS):
        res_send[j, :, 0:db] = res_ref[:, j * db : (j + 1) * db]
        res_send[j, :, db : db + LANES] = mine.astype(BF16)
    res_recv[c] = res_send[c]
    ctx_recv[me] = ctx_send[k]

    def ctx_copy(i):
        to = lax.rem(me + i, n)
        return remote(
            ctx_send.at[to // COLS], ctx_recv.at[me], ctx_ssem.at[i], ctx_rsem.at[i], to
        )

    def res_copy(i):
        to = lax.rem(c + i, COLS)
        return remote(
            res_send.at[to], res_recv.at[c], res_ssem.at[i], res_rsem.at[i], k * COLS + to
        )

    def part_copy(h, i):
        to = xor(k, i)
        return remote(
            part_send.at[h, to],
            part_recv.at[h, i],
            part_ssem.at[h, i],
            part_rsem.at[h, i],
            to * COLS + c,
        )

    pl.semaphore_wait(barrier, n - 1)
    loop(1, n, lambda i: ctx_copy(i).start())
    load_o.wait()
    loop(1, n, lambda i: ctx_copy(i).wait_recv())
    for d in range(n):
        ctx_all[d * rows : (d + 1) * rows, :] = ctx_recv[d].astype(F32)
    lhs = ctx_all[...].astype(BF16)

    for h in range(HALVES):
        cols = slice(h * half, (h + 1) * half)
        part[:, cols] = dot(lhs, wo[:, cols])
        for b in range(splits):
            part_send[h, b] = part[b * blk : (b + 1) * blk, cols].astype(BF16)
        for i in range(1, splits):
            part_copy(h, i).start()
        if h == 0:
            loop(1, COLS, lambda i: res_copy(i).start())

    loop(1, COLS, lambda i: res_copy(i).wait_recv())
    for j in range(COLS):
        attended[j * rows : (j + 1) * rows, :] = res_recv[j, :, 0:db].astype(F32)
        extra[j * rows : (j + 1) * rows, :] = res_recv[j, :, db : db + LANES].astype(F32)
    mine_rows = pl.ds(pl.multiple_of(k * blk, blk), blk)

    def piece(h, col, i):
        return y_all[h].at[col, pl.ds(pl.multiple_of(xor(k, i) * blk, blk), blk)]

    def z_copy(h, i):
        at = piece(h, c, 0)
        return remote(at, at, z_ssem.at[h, i], z_rsem.at[h, i], xor(k, i) * COLS + c)

    def y_copy(h, i):
        at = piece(h, c, i)
        return remote(at, at, y_ssem.at[h, i], y_rsem.at[h, i], k * COLS + across)

    def c_copy(h, far, i):
        at = piece(h, across if far else c, i)
        slot = splits * far + i
        return remote(at, at, c_ssem.at[h, slot], c_rsem.at[h, slot], k * COLS + beside)

    square = jnp.zeros((blk, 1), F32)
    for h in range(HALVES):
        cols = slice(h * half, (h + 1) * half)
        total = attended[:, cols] + part[mine_rows, cols]
        for i in range(1, splits):
            part_copy(h, i).wait_recv()
            total = total + part_recv[h, i].astype(F32)
        attended[:, cols] = total
        gain = gain_ref[:, pl.ds(pl.multiple_of(c * db + h * half, LANES), half)]
        square = square + jnp.sum(total * total, axis=-1, keepdims=True)
        y_all[h][c, mine_rows, 0:half] = (total * gain).astype(BF16)
        if h == HALVES - 1:
            high = square.astype(BF16).astype(F32)
            lane = lax.broadcasted_iota(jnp.int32, (blk, LANES), 1)
            packed = jnp.where(lane == 0, high, jnp.where(lane == 1, square - high, extra[...]))
            y_all[h][c, mine_rows, half : half + LANES] = packed.astype(BF16)
        for i in range(1, splits):
            z_copy(h, i).start()
        y_copy(h, 0).start()
        c_copy(h, 0, 0).start()

    def forward_z(h, i):
        z_copy(h, i).wait_recv()
        y_copy(h, i).start()
        c_copy(h, 0, i).start()

    def forward_y(h, i):
        y_copy(h, i).wait_recv()
        c_copy(h, 1, i).start()

    def chunk(h, i):
        if h == 0:
            load_g[i].wait()
            load_u[i].wait()
        lhs = y_all[h][plane[i], :, 0:half]
        at = pl.ds(pl.multiple_of(plane[i] * db + h * half, half), half)
        return dot(lhs, wg[at, :]), dot(lhs, wu[at, :])

    def arrive(h, far):
        for i in range(splits):
            c_copy(h, far, i).wait_recv()

    for i in range(1, splits):
        forward_z(0, i)
    gate, up = chunk(0, 0)
    forward_y(0, 0)
    for i in range(1, splits):
        forward_z(1, i)
        forward_y(0, i)
    arrive(0, 0)
    for h, i in ((0, 1), (1, 0), (0, 2)):
        g, u = chunk(h, i)
        gate, up = gate + g, up + u
    for i in range(splits):
        forward_y(1, i)
    arrive(0, 1)
    g, u = chunk(0, 3)
    gate, up = gate + g, up + u
    arrive(1, 0)
    for i in (1, 2):
        g, u = chunk(1, i)
        gate, up = gate + g, up + u
    arrive(1, 1)
    g, u = chunk(1, 3)
    gate, up = gate + g, up + u
    lane = lax.broadcasted_iota(jnp.int32, (all_rows, LANES), 1)
    square = jnp.zeros((all_rows, 1), F32)
    for j in range(COLS):
        tail = y_second[j, :, half : half + LANES].astype(F32)
        square = square + jnp.sum(jnp.where(lane < 2, tail, 0.0), axis=-1, keepdims=True)
    expert = k // (splits // EXPERTS)
    weight = jnp.sum(jnp.where(lane == expert + 2, tail, 0.0), axis=-1, keepdims=True)
    scale = lax.rsqrt(square * (1.0 / width) + 1e-5)
    gate = gate * scale
    hidden = gate / (1.0 + jnp.exp(-gate)) * (up * scale)
    hid_all[c] = hidden.astype(BF16)

    def hid_copy(i):
        at = hid_all.at[across if i == 3 else c]
        to = across if i == 2 else beside
        return remote(at, at, hid_ssem.at[i], hid_rsem.at[i], k * COLS + to)

    hid_copy(2).start()
    hid_copy(1).start()
    load_d[0].wait()
    acc[...] = dot(hid_all[c], wd[span(0, ff), :])
    load_d[1].wait()
    hid_copy(1).wait_recv()
    acc[...] += dot(hid_all[beside], wd[span(1, ff), :])
    hid_copy(2).wait_recv()
    hid_copy(3).start()
    load_d[2].wait()
    acc[...] += dot(hid_all[across], wd[span(2, ff), :])
    load_d[3].wait()
    hid_copy(3).wait_recv()

    def fin_copy(h, i):
        to = lax.rem(me + i, n)
        return remote(
            fin_send.at[h, to], fin_recv.at[h, me], fin_ssem.at[h, i], fin_rsem.at[h, i], to
        )

    for h in range(HALVES):
        cols = slice(h * half, (h + 1) * half)
        acc[:, cols] = (acc[:, cols] + dot(hid_all[corner], wd[span(3, ff), cols])) * weight
        acc[mine_rows, cols] = acc[mine_rows, cols] + attended[:, cols]
        for d in range(n):
            fin_send[h, d] = acc[d * rows : (d + 1) * rows, cols].astype(BF16)
        loop(1, n, lambda i: fin_copy(h, i).start())
        fin_recv[h, me] = fin_send[h, me]
    for h in range(HALVES):
        loop(1, n, lambda i: fin_copy(h, i).wait_recv())
        for j in range(COLS):
            total = fin_recv[h, j].astype(F32)
            for b in range(1, splits):
                total = total + fin_recv[h, b * COLS + j].astype(F32)
            out_ref[:, j * db + h * half : j * db + (h + 1) * half] = total.astype(BF16)

    loop(1, n, lambda i: ctx_copy(i).wait_send())
    loop(1, COLS, lambda i: res_copy(i).wait_send())
    for i in range(1, COLS):
        hid_copy(i).wait_send()
    for h in range(HALVES):
        loop(1, n, lambda i: fin_copy(h, i).wait_send())
        for i in range(splits):
            if i:
                part_copy(h, i).wait_send()
                z_copy(h, i).wait_send()
            y_copy(h, i).wait_send()
            c_copy(h, 0, i).wait_send()
            c_copy(h, 1, i).wait_send()


def body(
    queries,
    cache_keys,
    cache_values,
    row_lengths,
    residual,
    out_weight,
    norm_gain,
    expert_ids,
    gate_scores,
    gate_weight,
    up_weight,
    down_weight,
):
    n = lax.axis_size("dev")
    splits = n // COLS
    rows = queries.shape[0]
    head_dim = cache_keys.shape[2]
    heads = queries.shape[1] // head_dim
    kb, db = out_weight.shape[1:]
    ff = gate_weight.shape[1]
    all_rows = rows * n
    blk = rows * COLS
    half = db // HALVES
    vmem = pl.BlockSpec(memory_space=pltpu.VMEM)
    hbm = pl.BlockSpec(memory_space=pltpu.HBM)

    def dma(*count):
        return pltpu.SemaphoreType.DMA(count)

    return pl.pallas_call(
        functools.partial(kernel, n),
        out_shape=jax.ShapeDtypeStruct(residual.shape, BF16),
        in_specs=[hbm] * 12,
        out_specs=vmem,
        scratch_shapes=[
            pltpu.VMEM(queries.shape, BF16),
            pltpu.SMEM(row_lengths.shape, jnp.int32),
            pltpu.VMEM(residual.shape, BF16),
            pltpu.VMEM((1, norm_gain.shape[0]), F32),
            pltpu.VMEM(expert_ids.shape, jnp.int32),
            pltpu.VMEM(gate_scores.shape, F32),
            pltpu.VMEM(cache_keys.shape, BF16),
            pltpu.VMEM(cache_values.shape, BF16),
            pltpu.VMEM((kb, db), BF16),
            pltpu.VMEM(gate_weight.shape, BF16),
            pltpu.VMEM(up_weight.shape, BF16),
            pltpu.VMEM(down_weight.shape[1:], BF16),
            pltpu.VMEM((heads * rows, head_dim), F32),
            pltpu.VMEM((splits, rows, kb), BF16),
            pltpu.VMEM((n, rows, kb), BF16),
            pltpu.VMEM((all_rows, kb), F32),
            pltpu.VMEM((COLS, rows, db + LANES), BF16),
            pltpu.VMEM((COLS, rows, db + LANES), BF16),
            pltpu.VMEM((blk, LANES), F32),
            pltpu.VMEM((all_rows, db), F32),
            pltpu.VMEM((HALVES, splits, blk, half), BF16),
            pltpu.VMEM((HALVES, splits, blk, half), BF16),
            pltpu.VMEM((blk, db), F32),
            pltpu.VMEM((COLS, all_rows, half), BF16),
            pltpu.VMEM((COLS, all_rows, half + LANES), BF16),
            pltpu.VMEM((COLS, all_rows, ff), BF16),
            pltpu.VMEM((all_rows, db), F32),
            pltpu.VMEM((HALVES, n, rows, half), BF16),
            pltpu.VMEM((HALVES, n, rows, half), BF16),
            dma(6),
            dma(2 * rows),
            dma(13),
            dma(n),
            dma(n),
            dma(COLS),
            dma(COLS),
        ]
        + [dma(HALVES, splits)] * 6
        + [dma(HALVES, 2 * splits)] * 2
        + [dma(COLS)] * 2
        + [dma(HALVES, n)] * 2,
        compiler_params=pltpu.CompilerParams(
            collective_id=0, has_side_effects=True, vmem_limit_bytes=60 * 1024 * 1024
        ),
        name="layer",
    )(
        queries,
        row_lengths,
        residual,
        norm_gain[None, :],
        expert_ids,
        gate_scores,
        cache_keys,
        cache_values,
        out_weight,
        gate_weight,
        up_weight,
        down_weight,
    )


def solution(mesh):
    return jax.shard_map(
        body,
        mesh=mesh,
        in_specs=(
            P(("group", "dev"), None),
            P(("group", "dev"), None, None),
            P(("group", "dev"), None, None),
            P(("group", "dev")),
            P(("group", "dev"), None),
            P("dev", None, None),
            P(),
            P(("group", "dev"), None),
            P(("group", "dev"), None),
            P(None, "dev"),
            P(None, "dev"),
            P("dev", None, None),
        ),
        out_specs=P(("group", "dev"), None),
        check_vma=False,
    )
```

time: 47 us -> 53 us (1.13)
  Pallas kernels: 44.9 us -> 51.4 us
    pallas_call x1, Pallas kernels: 44.9 us -> 51.4 us  [body(): pl.pallas_call(functools.partial(kernel, n), out_shape=jax.ShapeDtypeStru...]
where the time goes in v2:
time: 53 us; the launch traced here: 52.9 us
  Pallas kernels  51.4 us (97%)
  local copies, waits for them, and re-layouts  1.46 us (3%)
    pallas_call x1, Pallas kernels, body(): pl.pallas_call(functools.partial(kernel, n), out_shape=jax.ShapeDtypeStru...  51.4 us
    unnamed x1, local copies, waits for them, and re-layouts  1.46 us

profile of v2, /device:TPU:0, one launch (start us, length us, event | category | flops | bytes accessed | tf_op | source)
XLA Modules:
  0.0 52.9 jit_solution(5547138656516026690)
XLA Ops:
  0.0 51.4 %layer.1 = bf16[4,7168]{1,0:T(4,128)(2,1)} custom-call(bf16[4,4096]{1,0:T(4,128)(2,1)} %q_hbm.1, s32[4]{0:T(128)} %len_hbm.1, bf16[4,7168]{1,0:T(4,128)(2,1)} %res_hbm.1, f32[1,7168]{1,0:T(1,128)} %bitcast.1, s32[4,3]{1,0:T(4,128)} %ids_hbm.1, f32[4,3]{1,0:T(4,128)} %score_hbm.1, bf16[4,512,256]{2,1,0:T(8,128)(2,1)} %keys_hbm.1, ...), custom_call_target="tpu_custom_call" | custom-call | tf_op jit(solution)/shard_map/layer/pallas_call | solution.py:464
  51.4 1.5 %copy.14 = bf16[4,7168]{1,0:T(4,128)(2,1)} copy(bf16[4,7168]{1,0:T(4,128)(2,1)} %layer.1) | data formatting | bytes 114688

commit v3 on v2

--- a/solution.py
+++ b/solution.py
@@ -117,7 +117,6 @@
             device_id_type=pl.DeviceIdType.MESH,
         )
 
-    loop(1, n, greet)
 
     def remote(src, dst, ssem, rsem, dev):
         return pltpu.make_async_remote_copy(
@@ -183,6 +182,7 @@
         copy.start()
     for copy in small[2:]:
         copy.start()
+    loop(1, n, greet)
     load_o.start()
     for i in range(COLS):
         load_g[i].start()

time: 53 us -> 45.2 us (0.85)
  Pallas kernels: 51.4 us -> 43.5 us
    pallas_call x1, Pallas kernels: 51.4 us -> 43.5 us  [body(): pl.pallas_call(functools.partial(kernel, n), out_shape=jax.ShapeDtypeStru...]
where the time goes in v3:
time: 45.2 us; the launch traced here: 45 us
  Pallas kernels  43.5 us (96%)
  local copies, waits for them, and re-layouts  1.46 us (3%)
    pallas_call x1, Pallas kernels, body(): pl.pallas_call(functools.partial(kernel, n), out_shape=jax.ShapeDtypeStru...  43.5 us
    unnamed x1, local copies, waits for them, and re-layouts  1.46 us

profile of v3, /device:TPU:0, one launch (start us, length us, event | category | flops | bytes accessed | tf_op | source)
XLA Modules:
  0.0 45.0 jit_solution(6701531317865531512)
XLA Ops:
  0.0 43.5 %layer.1 = bf16[4,7168]{1,0:T(4,128)(2,1)} custom-call(bf16[4,4096]{1,0:T(4,128)(2,1)} %q_hbm.1, s32[4]{0:T(128)} %len_hbm.1, bf16[4,7168]{1,0:T(4,128)(2,1)} %res_hbm.1, f32[1,7168]{1,0:T(1,128)} %bitcast.1, s32[4,3]{1,0:T(4,128)} %ids_hbm.1, f32[4,3]{1,0:T(4,128)} %score_hbm.1, bf16[4,512,256]{2,1,0:T(8,128)(2,1)} %keys_hbm.1, ...), custom_call_target="tpu_custom_call" | custom-call | tf_op jit(solution)/shard_map/layer/pallas_call | solution.py:464
  43.6 1.5 %copy.14 = bf16[4,7168]{1,0:T(4,128)(2,1)} copy(bf16[4,7168]{1,0:T(4,128)(2,1)} %layer.1) | data formatting | bytes 114688
